TPU v7x, 32 devices: a whole 2x2x4 slice. The times are simulated.
32 devices in a mesh: shot: 4 (over y, x), frame: 8 (over z, core).
Axes of the slice: x: 2, y: 2, z: 4, core: 2. Of those that a mesh axis runs over, the one named last changes fastest.
Arguments:
- queries: bfloat16 [16384, 768], P(('shot', 'frame')), may hold values from -20 to 20
- cotangent: bfloat16 [16384, 768], P(('shot', 'frame')), may hold values from -6 to 6
- ref_keys: bfloat16 [4, 8, 256, 768], P('shot', 'frame'), may hold values from -20 to 20
- ref_values: bfloat16 [4, 8, 256, 768], P('shot', 'frame'), may hold values from -6 to 6
- key_gain: float32 [768], replicated, may hold values from 0.1 to 1.9
- owners: int32 [4, 2], P('shot'), may hold values from 0 to 7, as said below
- counts: int32 [4, 2], P('shot'), may hold values from 128 to 256
Outputs:
- grad_queries: bfloat16 [16384, 768], P(('shot', 'frame'))
- grad_ref_keys: bfloat16 [4, 8, 256, 768], P('shot', 'frame')
- grad_ref_values: bfloat16 [4, 8, 256, 768], P('shot', 'frame')
- grad_gain: float32 [768], replicated
Inputs may be any that keep to these rules, and one draw needn't show every extreme that they name: `owners`: each shot's two owner indices differ.
All inputs are finite; a program needn't handle non-finite values.
Results may differ from a plain program's by a relative error of at most 0.0076.
Values may be sent and summed in bfloat16 or wider, within the bound.
A program may use at most 64 MiB of HBM per device.

v0:
```python
import jax
import jax.numpy as jnp
from jax import lax
from jax.sharding import PartitionSpec as P

HEADS = 6
DH = 128


def spread(value, axis, root):
    mine = lax.axis_index(axis) == root
    return lax.psum(jnp.where(mine, value, jnp.zeros_like(value)), axis)


def normalize(key_raw):
    shaped = key_raw.astype(jnp.float32).reshape(key_raw.shape[:-1] + (HEADS, DH))
    inverse = lax.rsqrt(jnp.mean(shaped * shaped, axis=-1, keepdims=True) + 1e-06)
    return (shaped * inverse, inverse)


def norm_backward(grad_normed, unit_keys, inverse, key_gain):
    grad_heads = grad_normed.reshape(unit_keys.shape)
    grad_unit = grad_heads * key_gain.reshape(HEADS, DH)
    grad_raw = inverse * (
        grad_unit - unit_keys * jnp.mean(grad_unit * unit_keys, axis=-1, keepdims=True)
    )
    gain_terms = jnp.sum(
        (grad_heads * unit_keys).reshape(grad_normed.shape[0], -1, HEADS * DH), axis=1
    )
    return (grad_raw.reshape(grad_normed.shape), gain_terms)


def local(queries, cotangent, ref_keys, ref_values, key_gain, owners, counts):
    my_frame = lax.axis_index("frame")
    tokens, width = queries.shape
    score_scale = DH ** (-0.5)
    fetched_keys = []
    fetched_values = []
    for which in range(2):
        got_keys, got_values = (
            spread(ref_keys[0, 0], "frame", owners[0, which]),
            spread(ref_values[0, 0], "frame", owners[0, which]),
        )
        fetched_keys.append(got_keys)
        fetched_values.append(got_values)
    key_raw = jnp.stack(fetched_keys)
    ref_rows = key_raw.shape[1]
    unit_keys, inverse = normalize(key_raw)
    keys = (
        (unit_keys * key_gain.reshape(HEADS, DH))
        .reshape(2 * ref_rows, HEADS, DH)
        .astype(jnp.bfloat16)
    )
    values = jnp.stack(fetched_values).reshape(2 * ref_rows, HEADS, DH)
    usable = (jnp.arange(ref_rows)[None, :] < counts[0][:, None]).reshape(2 * ref_rows)
    query_heads = queries.reshape(tokens, HEADS, DH)
    grad_heads = cotangent.reshape(tokens, HEADS, DH)
    scores = (
        jnp.einsum("thd,khd->htk", query_heads, keys, preferred_element_type=jnp.float32)
        * score_scale
    )
    scores = jnp.where(usable[None, None, :], scores, -1e30)
    highest = jnp.max(scores, axis=-1, keepdims=True)
    weights = jnp.exp(scores - highest)
    probs = weights / jnp.sum(weights, axis=-1, keepdims=True)
    probs_low = probs.astype(jnp.bfloat16)
    value_part = jnp.einsum(
        "htk,thd->khd", probs_low, grad_heads, preferred_element_type=jnp.float32
    )
    grad_probs = jnp.einsum("thd,khd->htk", grad_heads, values, preferred_element_type=jnp.float32)
    grad_scores = (
        probs * (grad_probs - jnp.sum(probs * grad_probs, axis=-1, keepdims=True)) * score_scale
    )
    grad_low = grad_scores.astype(jnp.bfloat16)
    grad_queries = (
        jnp.einsum("htk,khd->thd", grad_low, keys, preferred_element_type=jnp.float32)
        .reshape(tokens, width)
        .astype(jnp.bfloat16)
    )
    key_part = jnp.einsum("htk,thd->khd", grad_low, query_heads, preferred_element_type=jnp.float32)
    key_part = key_part.reshape(2, ref_rows, width)
    value_part = value_part.reshape(2, ref_rows, width)
    owned = owners[0] == my_frame
    key_sums, value_sums = lax.psum((key_part, value_part), "frame")
    grad_raw, gain_terms = norm_backward(key_sums, unit_keys, inverse, key_gain)
    gain_term = jnp.sum(jnp.where(owned[:, None], gain_terms, 0.0), axis=0)
    key_full = grad_raw.astype(jnp.bfloat16)
    value_full = value_sums.astype(jnp.bfloat16)
    nothing = jnp.zeros((), jnp.bfloat16)
    key_out = jnp.where(owned[0], key_full[0], jnp.where(owned[1], key_full[1], nothing))
    value_out = jnp.where(owned[0], value_full[0], jnp.where(owned[1], value_full[1], nothing))
    grad_gain = lax.psum(gain_term, ("shot", "frame"))
    return (
        grad_queries,
        key_out.reshape(1, 1, ref_rows, width),
        value_out.reshape(1, 1, ref_rows, width),
        grad_gain,
    )


def solution(mesh):
    in_specs = (
        P(("shot", "frame"), None),
        P(("shot", "frame"), None),
        P("shot", "frame", None, None),
        P("shot", "frame", None, None),
        P(),
        P("shot", None),
        P("shot", None),
    )
    out_specs = (
        P(("shot", "frame"), None),
        P("shot", "frame", None, None),
        P("shot", "frame", None, None),
        P(),
    )
    return jax.shard_map(local, mesh=mesh, in_specs=in_specs, out_specs=out_specs, check_vma=False)
```

profile of v0, /device:TPU:0, one launch (start us, length us, event | category | flops | bytes accessed | tf_op | source)
XLA Modules:
  0.0 254.6 jit_solution(5084655177389583921)
XLA Ops:
  7.2 0.0 copy-start.9
  7.2 0.0 all-reduce.7.cloned.1.call-start
  7.2 1.2 copy.66
  8.5 1.3 fusion.39
  11.1 1.2 copy.72
  12.3 0.9 select_bitcast_fusion.3
  13.2 0.9 select_bitcast_fusion.1
  14.1 0.0 all-reduce.7.cloned.1.call-update
  14.2 0.0 all-reduce.5.cloned.1.call-start
  14.2 2.3 copy.75
  16.5 0.1 iota_compare_fusion
  16.6 0.5 lt.26
  17.1 1.2 copy.69
  18.3 0.6 fusion.38
  19.0 0.5 fusion.51
  19.4 59.8 %all-reduce.7.cloned.1.call-done = (bf16[256,768]{0,1:T(8,128)(2,1)}, bf16[256,768]{0,1:T(8,128)(2,1)}, bf16[1,256,768]{1,2,0:T(8,128)(2,1)}, bf16[1,256,768]{1,2,0:T(8,128)(2,1)}) async-done(((bf16[256,768]{0,1:T(8,128)(2,1)}, bf16[256,768]{0,1:T(8,128)(2,1)}, bf16[1,256,768]{1,2,0:T(8,128)(2,1)}, bf16[1,256,768]{1,2,0:T(8,128)(2,1)}), (bf16[256,768]{0,1:T(8,128)(2,1)}, bf16[256,768]{0,1:T(8,128)(2,1)}, ...) | async-done | bytes 1572880 | tf_op jit(solution)/shard_map/psum | solution.py:12
  79.3 1.3 maximum_convert_fusion
  80.6 1.9 multiply_reduce_fusion.2
  82.5 0.5 copy.68
  82.9 0.7 add_rsqrt_fusion
  83.7 1.1 pad_maximum_fusion
  84.7 0.0 copy-start.8
  84.7 0.8 copy.74
  85.6 0.0 copy-start.12
  85.6 0.5 reshape.168
  86.1 4.9 %fusion.41 = f32[6,512,512]{2,1,0:T(8,128)} fusion(bf16[512,6,128]{0,2,1:T(8,128)(2,1)S(1)} %reshape.168, bf16[512,6,128]{0,2,1:T(8,128)(2,1)} %bitcast.121), kind=kOutput, calls=%fused_computation.63 | convolution fusion | flops 402653184 | bytes 7864320 | tf_op jit(solution)/shard_map/thd,khd->htk/dot_general | solution.py:70
  91.0 0.5 fusion.20
  91.5 4.9 %fusion.40 = (f32[6,512]{1,0:T(8,128)S(1)}, f32[6,512,512]{1,2,0:T(8,128)}) fusion(pred[512]{0:T(512)(128)(4,1)S(1)} %copy-done.12, bf16[512,6,128]{2,0,1:T(8,128)(2,1)S(1)} %fusion.20, bf16[512,6,128]{0,2,1:T(8,128)(2,1)S(1)} %bitcast.123), kind=kOutput, calls=%fused_computation.62 | convolution fusion | flops 408945152 | bytes 7877120 | tf_op jit(solution)/shard_map/sub | solution.py:64
  96.4 5.0 %fusion.22 = f32[512,6,128]{2,0,1:T(8,128)} fusion(bf16[512,6,128]{0,2,1:T(8,128)(2,1)S(1)} %bitcast.122, f32[6,512,512]{1,2,0:T(8,128)} %get-tuple-element.35, f32[6,512]{1,0:T(8,128)S(1)} %get-tuple-element.34), kind=kOutput, calls=%fused_computation.33 | convolution fusion | flops 405798912 | bytes 8663040 | tf_op jit(solution)/shard_map/htk,thd->khd/dot_general | solution.py:67
  101.4 10.8 %fusion.21 = f32[512,6,128]{2,0,1:T(8,128)S(1)} fusion(bf16[512,6,128]{0,2,1:T(8,128)(2,1)S(1)} %bitcast.124, f32[6,512,512]{2,1,0:T(8,128)} %fusion.41, f32[6,512,512]{1,2,0:T(8,128)} %get-tuple-element.35, f32[6,512]{1,0:T(8,128)S(1)} %get-tuple-element.34), kind=kOutput, calls=%fused_computation.32 | convolution fusion | flops 413666816 | bytes 14954496 | tf_op jit(solution)/shard_map/htk,thd->khd/dot_general | solution.py:80
  112.2 0.5 copy.81
  112.6 1.0 reshape.170
  113.6 1.3 copy.82
  114.9 0.0 all-reduce.5.cloned.1.call-update
  114.9 1.9 copy.84
  116.8 1.0 reshape.172
  117.8 0.1 copy.85
  118.0 71.7 %all-reduce.8 = bf16[2,256,768]{1,2,0:T(8,128)(2,1)S(1)} all-reduce(f32[2,256,768]{1,2,0:T(8,128)S(1)} %copy.85), channel_id=1, replica_groups=mesh['shot'=4,'frame'=8] {'frame'}, use_global_device_ids=true, to_apply=%region_10.11 | all-reduce | flops 393216 | bytes 2359296 | tf_op jit(solution)/shard_map/psum | solution.py:84
  189.6 11.2 %fusion.25 = bf16[6,128,512]{2,1,0:T(8,128)(2,1)S(1)} fusion(bf16[512,6,128]{2,0,1:T(8,128)(2,1)} %copy-done.6, f32[6,512,512]{2,1,0:T(8,128)} %fusion.41, f32[6,512,512]{1,2,0:T(8,128)} %get-tuple-element.35, f32[6,512]{1,0:T(8,128)S(1)} %get-tuple-element.34), kind=kOutput, calls=%fused_computation.34 | convolution fusion | flops 414060032 | bytes 14168064 | tf_op jit(solution)/shard_map/htk,khd->thd/dot_general | solution.py:76
  200.8 1.2 copy.86
  202.0 1.3 fusion.29
  203.3 0.9 copy.88
  204.2 1.7 multiply_reduce_fusion.1
  205.9 2.0 multiply_reduce_fusion
  208.0 1.3 fusion.31
  209.3 0.9 copy.87
  210.2 0.1 select_reduce_fusion
  210.3 37.5 %psum.55 = f32[768]{0:T(1024)} all-reduce(f32[768]{0:T(1024)S(1)} %select_reduce_fusion), channel_id=1, replica_groups=mesh['shot'=4,'frame'=8] {'shot','frame'}, use_global_device_ids=true, to_apply=%region_13.14 | all-reduce | flops 768 | bytes 6144 | tf_op jit(solution)/shard_map/psum | solution.py:92
  (26 shorter events, 0.1 us)
Async XLA Ops:
  7.2 11.2 %copy-start.9 = (s32[1,2]{1,0:T(1,128)S(1)}, s32[1,2]{1,0:T(1,128)}, u32[]{:S(2)}) copy-start(s32[1,2]{1,0:T(1,128)} %param.12) | copy-start | bytes 28
  7.2 9.3 %copy-start.11 = (s32[1,2]{1,0:T(1,128)S(1)}, s32[1,2]{1,0:T(1,128)}, u32[]{:S(2)}) copy-start(s32[1,2]{1,0:T(1,128)} %param.13) | copy-start | bytes 28
  7.2 9.9 %copy-start.3 = (bf16[512,768]{1,0:T(8,128)(2,1)S(1)}, bf16[512,768]{1,0:T(8,128)(2,1)}, u32[]{:S(2)}) copy-start(bf16[512,768]{1,0:T(8,128)(2,1)} %param.7) | copy-start | bytes 2359300
  7.2 72.1 %all-reduce.7.cloned.1.call-start = ((), (), s32[]{:S(2)}) async-start(), calls=%async_computation.1 | async-start | bytes 3145728 | tf_op jit(solution)/shard_map/psum | solution.py:12
  14.2 190.1 %all-reduce.5.cloned.1.call-start = ((), (), s32[]{:S(2)}) async-start(), calls=%async_computation | async-start | bytes 3145728 | tf_op jit(solution)/shard_map/psum | solution.py:84
  79.3 4.4 %copy-start.7 = (bf16[1,256,768]{1,2,0:T(8,128)(2,1)S(1)}, bf16[1,256,768]{1,2,0:T(8,128)(2,1)}, u32[]{:S(2)}) copy-start(bf16[1,256,768]{1,2,0:T(8,128)(2,1)} %get-tuple-element.22) | copy-start | bytes 1179652
  84.7 6.2 %copy-start.8 = (f32[768]{0:T(1024)S(1)}, f32[768]{0:T(1024)}, u32[]{:S(2)}) copy-start(f32[768]{0:T(1024)} %param.11) | copy-start | bytes 9220
  85.6 5.9 %copy-start.12 = (pred[512]{0:T(512)(128)(4,1)S(1)}, pred[512]{0:T(512)(128)(4,1)}, u32[]{:S(2)}) copy-start(pred[512]{0:T(512)(128)(4,1)} %lt.26) | copy-start | bytes 1540
  86.1 5.4 %copy-start.4 = (bf16[512,768]{0,1:T(8,128)(2,1)S(1)}, bf16[512,768]{0,1:T(8,128)(2,1)}, u32[]{:S(2)}) copy-start(bf16[512,768]{0,1:T(8,128)(2,1)} %copy.69) | copy-start | bytes 2359300
  91.5 4.9 %copy-start.6 = (bf16[512,6,128]{2,0,1:T(8,128)(2,1)}, bf16[512,6,128]{2,0,1:T(8,128)(2,1)S(1)}, u32[]{:S(2)}) copy-start(bf16[512,6,128]{2,0,1:T(8,128)(2,1)S(1)} %fusion.20) | copy-start | bytes 2359300
  91.5 4.9 %copy-start.2 = (bf16[512,768]{0,1:T(8,128)(2,1)S(1)}, bf16[512,768]{0,1:T(8,128)(2,1)}, u32[]{:S(2)}) copy-start(bf16[512,768]{0,1:T(8,128)(2,1)} %copy.75) | copy-start | bytes 2359300
  96.4 5.0 %copy-start.5 = (bf16[512,768]{0,1:T(8,128)(2,1)S(1)}, bf16[512,768]{0,1:T(8,128)(2,1)}, u32[]{:S(2)}) copy-start(bf16[512,768]{0,1:T(8,128)(2,1)} %copy.69) | copy-start | bytes 2359300
  189.6 14.6 %copy-start = (bf16[256,768]{0,1:T(8,128)(2,1)S(1)}, bf16[256,768]{0,1:T(8,128)(2,1)}, u32[]{:S(2)}) copy-start(bf16[256,768]{0,1:T(8,128)(2,1)} %get-tuple-element.20) | copy-start | bytes 1179652
  189.6 14.6 %copy-start.1 = (bf16[256,768]{0,1:T(8,128)(2,1)S(1)}, bf16[256,768]{0,1:T(8,128)(2,1)}, u32[]{:S(2)}) copy-start(bf16[256,768]{0,1:T(8,128)(2,1)} %get-tuple-element.21) | copy-start | bytes 1179652
  200.8 9.3 %copy-start.10 = (pred[2]{0:T(512)(128)(4,1)S(1)}, pred[2]{0:T(512)(128)(4,1)}, u32[]{:S(2)}) copy-start(pred[2]{0:T(512)(128)(4,1)} %fusion.51) | copy-start | bytes 10
Sparse Core Ops, SparseCore 0:
  14.3 64.9 all-reduce.6
  115.1 70.9 all-reduce.4
where the time goes:
time: 256 us; the launch traced here: 255 us
  blocking collectives  109 us (43%)
  waiting for transfers between devices  59.9 us (23%)
  matrix products  36.7 us (14%)
  local copies, waits for them, and re-layouts  18.9 us (7%)
  between operations  15.6 us (6%)
  other arithmetic  14.2 us (6%)
    psum x1, blocking collectives, local(): key_sums, value_sums = lax.psum((key_part, value_part), 'frame')  71.7 us
    psum x1, waiting for transfers between devices, spread(): return lax.psum(jnp.where(mine, value, jnp.zeros_like(value)), axis)  59.8 us
    psum x1, blocking collectives, local(): grad_gain = lax.psum(gain_term, ('shot', 'frame'))  37.5 us
    dot_general x1, matrix products, local(): jnp.einsum('htk,khd->thd', grad_low, keys, preferred_element_type=jnp.flo...  11.2 us
    dot_general x1, matrix products, local(): jnp.einsum('htk,thd->khd', grad_low, query_heads, preferred_element_type=...  10.8 us
    unnamed x33, local copies, waits for them, and re-layouts  8.95 us
  transfers between devices with their start and end apart: 2, of which 1 were waited for; matrix products, arithmetic and copies ran while one was open for 9% of the time, Pallas kernels for 0%

commit v1 on v0

v1 whole, which is shorter than its diff:
```python
import functools

import jax
import jax.numpy as jnp
from jax import lax
from jax.experimental import pallas as pl
from jax.experimental.pallas import tpu as pltpu
from jax.sharding import PartitionSpec as P

HEADS = 6
DH = 128
HALF = HEADS // 2
WIDE = HALF * DH
SCALE = DH ** (-0.5)
LOG2E = 1.4426950408889634
F32 = jnp.float32
BF16 = jnp.bfloat16


def dot(a, b, ca, cb):
    return lax.dot_general(a, b, (((ca,), (cb,)), ((), ())), preferred_element_type=F32)


def kernel(
    chips, owners, counts, q, g, rk, rv, gain,
    gq_out, ok_out, ov_out, gain_out,
    qh, gh, pkv, buf, kn, vn, acc, rbuf, fin, gqs, outs,
    xs, xr, bs, br, rs, rr, fs, fr, gs, gr, os_, or_,
):
    shot = lax.axis_index("shot")
    me = lax.axis_index("frame")
    z = me // 2
    core = me % 2
    peer = z * 2 + 1 - core
    tokens, rows = q.shape[0], rk.shape[0]
    block = min(256, tokens)
    last = chips - 1

    def dev(frame):
        return (shot, frame)

    def remote(src, dst, s, r, frame):
        return pltpu.make_async_remote_copy(
            src_ref=src, dst_ref=dst, send_sem=s, recv_sem=r,
            device_id=dev(frame), device_id_type=pl.DeviceIdType.MESH,
        )

    barrier = pltpu.get_barrier_semaphore()
    pl.semaphore_signal(barrier, inc=1, device_id=dev(peer), device_id_type=pl.DeviceIdType.MESH)

    @pl.when(z > 0)
    def _():
        pl.semaphore_signal(barrier, inc=1, device_id=dev(me - 2), device_id_type=pl.DeviceIdType.MESH)

    @pl.when(z < last)
    def _():
        pl.semaphore_signal(barrier, inc=1, device_id=dev(me + 2), device_id_type=pl.DeviceIdType.MESH)

    pl.semaphore_wait(barrier, 1 + jnp.where(z > 0, 1, 0) + jnp.where(z < last, 1, 0))

    own = [owners[0], owners[1]]
    far = (z * 2 >= chips).astype(jnp.int32)
    base = core * WIDE

    def cols(h):
        return pl.ds(pl.multiple_of(base + h * DH, DH), DH)

    mine_cols = pl.ds(pl.multiple_of(base, DH), WIDE)
    peer_cols = pl.ds(pl.multiple_of((1 - core) * WIDE, DH), WIDE)

    def way(d):
        pos = jnp.where(d == 0, z, last - z)
        step = 2 - 4 * d
        return pos, me + step, me - step

    exchange = [
        remote(rk.at[:, peer_cols], pkv.at[0], xs.at[0], xr.at[0], peer),
        remote(rv.at[:, peer_cols], pkv.at[1], xs.at[1], xr.at[1], peer),
        remote(q.at[:, peer_cols], qh.at[core], xs.at[2], xr.at[2], peer),
        remote(g.at[:, peer_cols], gh.at[core], xs.at[3], xr.at[3], peer),
    ]
    landing = [
        exchange[0],
        exchange[1],
        remote(q.at[:, peer_cols], qh.at[1 - core], xs.at[2], xr.at[2], peer),
        remote(g.at[:, peer_cols], gh.at[1 - core], xs.at[3], xr.at[3], peer),
    ]
    for copy in exchange:
        copy.start()
    gain_out[...] = jnp.zeros_like(gain_out)
    qh[core] = q[:, mine_cols]
    gh[core] = g[:, mine_cols]
    landing[0].wait_recv()
    landing[1].wait_recv()

    def bcopy(d, h, kv, j, frame):
        slot = (h * 2 + kv) * 2 + j
        ref = buf.at[d, h, kv, j]
        return remote(ref, ref, bs.at[d, slot], br.at[d, slot], frame)

    def rcopy(d, h, kind, frame):
        slot = h * 2 + kind
        return remote(acc.at[h, kind, d], rbuf.at[d, h, kind], rs.at[d, slot], rr.at[d, slot], frame)

    def fcopy(d, h, kind, frame):
        slot = h * 2 + kind
        ref = fin.at[d, h, kind]
        return remote(ref, ref, fs.at[d, slot], fr.at[d, slot], frame)

    def gcopy(h, origin):
        return remote(gqs.at[h, origin], gq_out.at[:, cols(h)], gs.at[h], gr.at[h], peer)

    def ocopy(h, kind):
        dst = (ok_out, ov_out)[kind].at[:, cols(h)]
        slot = h * 2 + kind
        return remote(outs.at[h, kind], dst, os_.at[slot], or_.at[slot], peer)

    def spread(h):
        for turn in range(2):
            d = far if turn == 0 else 1 - far
            pos, after, _ = way(d)
            for kv in range(2):
                for j in range(2):
                    copy = bcopy(d, h, kv, j, after)
                    pl.when(pos > 0)(copy.wait_recv)
                    here = lax.select(own[j] == me, (rk, rv)[kv][:, cols(h)], pkv[kv, :, h * DH : (h + 1) * DH])
                    use = ((own[j] >= 2 * z) & (own[j] < 2 * z + 2)) | (pos == 0)
                    buf[d, h, kv, j] = lax.select(use, here, buf[d, h, kv, j])
                    pl.when(pos < last)(copy.start)

    def raw(h, kv, j, owner):
        return lax.select(owner < 2 * z + 2, buf[0, h, kv, j], buf[1, h, kv, j])

    def unit_of(key_raw):
        key_raw = key_raw.astype(F32)
        inverse = lax.rsqrt(jnp.mean(key_raw * key_raw, axis=-1, keepdims=True) + 1e-06)
        return key_raw * inverse, inverse

    row = lax.broadcasted_iota(jnp.int32, (2 * rows, 1), 0)
    usable = ((row < rows) & (row < counts[0])) | ((row >= rows) & (row < rows + counts[1]))

    def attend(h):
        for j in range(2):
            unit, _ = unit_of(raw(h, 0, j, own[j]))
            kn[j * rows : (j + 1) * rows] = (unit * gain[:, cols(h)]).astype(BF16)
            vn[j * rows : (j + 1) * rows] = raw(h, 1, j, own[j])
        if h == 0:
            landing[2].wait_recv()
            landing[3].wait_recv()
        acc[h] = jnp.zeros_like(acc[h])
        per = tokens // block

        @pl.loop(0, 2 * per)
        def _(i):
            origin, part = i // per, i % per
            at = pl.ds(pl.multiple_of(part * block, block), block)
            qb = qh[origin, at, h * DH : (h + 1) * DH]
            gb = gh[origin, at, h * DH : (h + 1) * DH]
            keys, values = kn[...], vn[...]
            scores = jnp.where(usable, dot(keys, qb, 1, 1), -1e30)
            highest = jnp.max(scores, axis=0, keepdims=True)
            weights = jnp.exp2((scores - highest) * (SCALE * LOG2E))
            inv = 1.0 / jnp.sum(weights, axis=0, keepdims=True)
            probs = weights * inv
            grad_probs = dot(values, gb, 1, 1)
            delta = jnp.sum(probs * grad_probs, axis=0, keepdims=True)
            grad_low = (probs * (grad_probs - delta) * SCALE).astype(BF16)
            gqs[h, origin, at] = dot(grad_low, keys, 0, 0).astype(BF16)
            acc[h, 0] += dot(grad_low, qb, 1, 0).reshape(2, rows, DH)
            acc[h, 1] += dot(probs.astype(BF16), gb, 1, 0).reshape(2, rows, DH)

        d = far
        pos, after, _ = way(d)
        for kind in range(2):
            pl.when(pos == 0)(rcopy(d, h, kind, after).start)
        gcopy(h, 1 - core).start()
        gq_out[:, cols(h)] = gqs[h, core]

    def finish(d, h, kind, before):
        total = acc[h, kind, d]
        if kind == 1:
            fin[d, h, 1] = total.astype(BF16)
        else:
            owner = jnp.where(d == 0, own[0], own[1])
            unit, inverse = unit_of(raw(h, 0, d, owner))
            grad_unit = total * gain[:, cols(h)]
            grad_raw = inverse * (grad_unit - unit * jnp.mean(grad_unit * unit, axis=-1, keepdims=True))
            fin[d, h, 0] = grad_raw.astype(BF16)
            gain_out[:, cols(h)] += jnp.sum(total * unit, axis=0, keepdims=True)
        fcopy(d, h, kind, before).start()

    def reduce(h):
        for turn in range(2):
            d = far if turn == 0 else 1 - far
            pos, after, before = way(d)

            @pl.when(pos > 0)
            def _():
                for kind in range(2):
                    copy = rcopy(d, h, kind, after)
                    copy.wait_recv()
                    acc[h, kind, d] += rbuf[d, h, kind]
                    pl.when(pos < last)(copy.start)
                    pl.when(pos == last)(functools.partial(finish, d, h, kind, before))

    def hand_back(h):
        for turn in range(2):
            d = 1 - far if turn == 0 else far
            pos, _, before = way(d)

            @pl.when(pos < last)
            def _():
                for kind in range(2):
                    copy = fcopy(d, h, kind, before)
                    copy.wait_recv()
                    pl.when(pos > 0)(copy.start)

        for kind in range(2):
            first, second = fin[0, h, kind], fin[1, h, kind]
            nothing = jnp.zeros_like(first)
            out = (ok_out, ov_out)[kind]
            out[:, cols(h)] = lax.select(own[0] == me, first, lax.select(own[1] == me, second, nothing))
            outs[h, kind] = lax.select(own[0] == peer, first, lax.select(own[1] == peer, second, nothing))
            ocopy(h, kind).start()

    for tick in range(HALF + 4):
        if tick < HALF:
            spread(tick)
        if 0 <= tick - 1 < HALF:
            attend(tick - 1)
        if 0 <= tick - 2 < HALF:
            reduce(tick - 2)
        if 0 <= tick - 3 < HALF:
            hand_back(tick - 3)

    for copy in exchange:
        copy.wait_send()
    for h in range(HALF):
        gcopy(h, 1 - core).wait()
        for kind in range(2):
            ocopy(h, kind).wait()
        for d in range(2):
            pos, after, before = way(d)

            @pl.when(pos < last)
            def _():
                for kind in range(2):
                    for j in range(2):
                        bcopy(d, h, kind, j, after).wait_send()
                    rcopy(d, h, kind, after).wait_send()

            @pl.when(pos > 0)
            def _():
                for kind in range(2):
                    fcopy(d, h, kind, before).wait_send()


def local(queries, cotangent, ref_keys, ref_values, key_gain, owners, counts):
    tokens, width = queries.shape
    rows = ref_keys.shape[2]
    chips = lax.axis_size("frame") // 2
    vmem = pl.BlockSpec(memory_space=pltpu.VMEM)
    smem = pl.BlockSpec(memory_space=pltpu.SMEM)
    dma = pltpu.SemaphoreType.DMA
    gq, ok, ov, gain = pl.pallas_call(
        functools.partial(kernel, chips),
        out_shape=(
            jax.ShapeDtypeStruct((tokens, width), BF16),
            jax.ShapeDtypeStruct((rows, width), BF16),
            jax.ShapeDtypeStruct((rows, width), BF16),
            jax.ShapeDtypeStruct((1, width), F32),
        ),
        in_specs=[smem, smem] + [vmem] * 5,
        out_specs=(vmem,) * 4,
        scratch_shapes=[
            pltpu.VMEM((2, tokens, WIDE), BF16),
            pltpu.VMEM((2, tokens, WIDE), BF16),
            pltpu.VMEM((2, rows, WIDE), BF16),
            pltpu.VMEM((2, HALF, 2, 2, rows, DH), BF16),
            pltpu.VMEM((2 * rows, DH), BF16),
            pltpu.VMEM((2 * rows, DH), BF16),
            pltpu.VMEM((HALF, 2, 2, rows, DH), F32),
            pltpu.VMEM((2, HALF, 2, rows, DH), F32),
            pltpu.VMEM((2, HALF, 2, rows, DH), BF16),
            pltpu.VMEM((HALF, 2, tokens, DH), BF16),
            pltpu.VMEM((HALF, 2, rows, DH), BF16),
            dma((4,)), dma((4,)),
            dma((2, HALF * 4)), dma((2, HALF * 4)),
            dma((2, HALF * 2)), dma((2, HALF * 2)),
            dma((2, HALF * 2)), dma((2, HALF * 2)),
            dma((HALF,)), dma((HALF,)),
            dma((HALF * 2,)), dma((HALF * 2,)),
        ],
        compiler_params=pltpu.CompilerParams(
            collective_id=0, has_side_effects=True, vmem_limit_bytes=48 * 1024 * 1024
        ),
    )(owners[0], counts[0], queries, cotangent, ref_keys[0, 0], ref_values[0, 0], key_gain[None, :])
    grad_gain = lax.psum(gain[0], ("shot", "frame"))
    return gq, ok[None, None], ov[None, None], grad_gain


def solution(mesh):
    in_specs = (
        P(("shot", "frame"), None),
        P(("shot", "frame"), None),
        P("shot", "frame", None, None),
        P("shot", "frame", None, None),
        P(),
        P("shot", None),
        P("shot", None),
    )
    out_specs = (
        P(("shot", "frame"), None),
        P("shot", "frame", None, None),
        P("shot", "frame", None, None),
        P(),
    )
    return jax.shard_map(local, mesh=mesh, in_specs=in_specs, out_specs=out_specs, check_vma=False)
```

time: 256 us -> 146 us (0.57)
  Pallas kernels: 0 us -> 98 us
  blocking collectives: 109 us -> 38.9 us
  waiting for transfers between devices: 59.9 us -> 0 us
  matrix products: 36.7 us -> 0 us
  between operations: 15.6 us -> 0.66 us
  other arithmetic: 14.2 us -> 0.02 us
  local copies, waits for them, and re-layouts: 18.9 us -> 7.98 us
    pallas_call x0 -> x1, Pallas kernels: none -> 98 us  [local(): pl.pallas_call(functools.partial(kernel, chips), out_shape=(jax.ShapeDtyp...]
    psum x2 -> x1, blocking collectives: 109 us -> 38.9 us  [local(): grad_gain = lax.psum(gain[0], ('shot', 'frame'))]
    psum x2 -> x0, waiting for transfers between devices: 59.8 us -> none  [the longest x1 59.8 us: spread(): return lax.psum(jnp.where(mine, value, jnp.zeros_like(value)), axis)]
    dot_general x4 -> x0, matrix products: 31.8 us -> none  [the longest x1 11.2 us: local(): jnp.einsum('htk,khd->thd', grad_low, keys, preferred_element_type=jnp.flo...]
    reduce_sum x4 -> x0, other arithmetic: 5.71 us -> none  [the longest x1 2.02 us: norm_backward(): jnp.sum((grad_heads * unit_keys).reshape(grad_normed.shape[0], -1, HEADS...]
    sub x1 -> x0, matrix products: 4.86 us -> none  [local(): weights = jnp.exp(scores - highest)]
    reshape x5 -> x0, local copies, waits for them, and re-layouts: 3.9 us -> none  [the longest x2 2.27 us: local(): key_part = key_part.reshape(2, ref_rows, width)]
    select_n x3 -> x0, other arithmetic: 3.5 us -> none  [the longest x1 1.28 us: local(): jnp.where(owned[0], value_full[0], jnp.where(owned[1], value_full[1], not...]
  transfers between devices with their start and end apart: 2 -> 0, of which waited for: 1 -> 0; matrix products, arithmetic and copies ran while one was open for 9% -> 0% of each run, Pallas kernels for 0% -> 0%
where the time goes in v1:
time: 146 us
  Pallas kernels  98 us (67%)
  blocking collectives  38.9 us (27%)
  local copies, waits for them, and re-layouts  7.98 us (5%)
    pallas_call x1, Pallas kernels, local(): pl.pallas_call(functools.partial(kernel, chips), out_shape=(jax.ShapeDtyp...  98 us
    psum x1, blocking collectives, local(): grad_gain = lax.psum(gain[0], ('shot', 'frame'))  38.9 us
    unnamed x17, local copies, waits for them, and re-layouts  7.97 us

profile of v1, /device:TPU:0, one launch (start us, length us, event | category | flops | bytes accessed | tf_op | source)
XLA Modules:
  0.0 145.5 jit_solution(4548362076391484835)
XLA Ops:
  0.6 0.0 copy-start.6
  0.6 0.7 copy-done.6
  1.3 0.0 copy-start.4
  1.3 0.0 copy-start.5
  1.3 0.6 copy-done.4
  2.0 0.0 copy-done.5
  2.0 0.0 copy-start
  2.0 1.1 copy-done
  3.1 0.0 copy-start.1
  3.1 1.1 copy-done.1
  4.3 0.0 copy-start.2
  4.3 1.0 copy-done.2
  5.3 0.0 copy-start.3
  5.3 1.0 copy-done.3
  6.3 98.0 %shard_map.102 = (bf16[512,768]{1,0:T(8,128)(2,1)S(1)}, bf16[256,768]{1,0:T(8,128)(2,1)S(1)}, bf16[256,768]{1,0:T(8,128)(2,1)S(1)}, f32[1,768]{1,0:T(1,128)S(1)}) custom-call(s32[2]{0:T(128)S(1)} %bitcast.10, s32[2]{0:T(128)S(1)} %bitcast.11, bf16[512,768]{1,0:T(8,128)(2,1)S(1)} %copy-done, bf16[512,768]{1,0:T(8,128)(2,1)S(1)} %copy-done.1, ...), custom_call_target="tpu_custom_call" | custom-call | tf_op jit(solution)/shard_map/pallas_call | solution.py:265
  104.3 38.9 %psum.7 = f32[768]{0:T(1024)} all-reduce(f32[768]{0:T(1024)S(1)} %reduce), channel_id=1, replica_groups=mesh['shot'=4,'frame'=8] {'shot','frame'}, use_global_device_ids=true, to_apply=%region_0.0 | all-reduce | flops 768 | bytes 6144 | tf_op jit(solution)/shard_map/psum | solution.py:298
  143.1 0.9 copy.14
  144.0 0.7 copy.15
  144.8 0.7 copy.16
  (2 shorter events, 0.0 us)
Async XLA Ops:
  0.6 0.7 copy-start.6
  1.3 0.7 copy-start.4
  1.3 0.7 copy-start.5
  2.0 1.1 copy-start
  3.1 1.1 copy-start.1
  4.3 1.0 copy-start.2
  5.3 1.0 copy-start.3

commit v2 on v1

--- a/solution.py
+++ b/solution.py
@@ -22,10 +22,10 @@
 
 
 def kernel(
-    chips, owners, counts, q, g, rk, rv, gain,
+    shots, chips, owners, counts, q, g, rk, rv, gain,
     gq_out, ok_out, ov_out, gain_out,
-    qh, gh, pkv, buf, kn, vn, acc, rbuf, fin, gqs, outs,
-    xs, xr, bs, br, rs, rr, fs, fr, gs, gr, os_, or_,
+    qh, gh, pkv, buf, kn, vn, acc, rbuf, fin, gqs, outs, parts, gsum, gmine,
+    xs, xr, bs, br, rs, rr, fs, fr, gs, gr, os_, or_, ps, pr, ts, tr, ms, mr,
 ):
     shot = lax.axis_index("shot")
     me = lax.axis_index("frame")
@@ -56,7 +56,10 @@
     def _():
         pl.semaphore_signal(barrier, inc=1, device_id=dev(me + 2), device_id_type=pl.DeviceIdType.MESH)
 
-    pl.semaphore_wait(barrier, 1 + jnp.where(z > 0, 1, 0) + jnp.where(z < last, 1, 0))
+    for turn in range(1, shots):
+        other = (lax.rem(shot + turn, shots), me)
+        pl.semaphore_signal(barrier, inc=1, device_id=other, device_id_type=pl.DeviceIdType.MESH)
+    pl.semaphore_wait(barrier, shots + jnp.where(z > 0, 1, 0) + jnp.where(z < last, 1, 0))
 
     own = [owners[0], owners[1]]
     far = (z * 2 >= chips).astype(jnp.int32)
@@ -87,7 +90,6 @@
     ]
     for copy in exchange:
         copy.start()
-    gain_out[...] = jnp.zeros_like(gain_out)
     qh[core] = q[:, mine_cols]
     gh[core] = g[:, mine_cols]
     landing[0].wait_recv()
@@ -114,6 +116,52 @@
         dst = (ok_out, ov_out)[kind].at[:, cols(h)]
         slot = h * 2 + kind
         return remote(outs.at[h, kind], dst, os_.at[slot], or_.at[slot], peer)
+
+    def pcopy(turn, slot):
+        return pltpu.make_async_remote_copy(
+            src_ref=parts.at[slot], dst_ref=parts.at[slot], send_sem=ps.at[turn], recv_sem=pr.at[turn],
+            device_id=(lax.rem(shot + turn, shots), me), device_id_type=pl.DeviceIdType.MESH,
+        )
+
+    def tcopy(d, frame):
+        return remote(gsum.at[d], gsum.at[d], ts.at[d], tr.at[d], frame)
+
+    gain_copy = remote(gmine, gain_out.at[:, mine_cols], ms.at[0], mr.at[0], peer)
+    ends = (z == 0) | (z == last)
+
+    def gain_start():
+        @pl.when(ends)
+        def _():
+            for turn in range(1, shots):
+                pcopy(turn, shot).start()
+
+    def gain_end():
+        @pl.when(ends)
+        def _():
+            for turn in range(1, shots):
+                pcopy(turn, lax.rem(shot - turn + shots, shots)).wait_recv()
+            total = parts[0]
+            for other in range(1, shots):
+                total += parts[other]
+            d = jnp.where(z == last, 0, 1)
+            gsum[d] = total
+            _, _, before = way(d)
+            tcopy(d, before).start()
+
+    def gain_back():
+        for turn in range(2):
+            d = 1 - far if turn == 0 else far
+            pos, _, before = way(d)
+
+            @pl.when(pos < last)
+            def _():
+                copy = tcopy(d, before)
+                copy.wait_recv()
+                pl.when(pos > 0)(copy.start)
+
+        gmine[...] = jnp.sum(gsum[0] + gsum[1], axis=0, keepdims=True)
+        gain_out[:, mine_cols] = gmine[...]
+        gain_copy.start()
 
     def spread(h):
         for turn in range(2):
@@ -186,7 +234,8 @@
             grad_unit = total * gain[:, cols(h)]
             grad_raw = inverse * (grad_unit - unit * jnp.mean(grad_unit * unit, axis=-1, keepdims=True))
             fin[d, h, 0] = grad_raw.astype(BF16)
-            gain_out[:, cols(h)] += jnp.sum(total * unit, axis=0, keepdims=True)
+            terms = jnp.sum((total * unit).reshape(rows // 8, 8, DH), axis=0)
+            parts[shot, :, h * DH : (h + 1) * DH] = terms
         fcopy(d, h, kind, before).start()
 
     def reduce(h):
@@ -230,8 +279,19 @@
             attend(tick - 1)
         if 0 <= tick - 2 < HALF:
             reduce(tick - 2)
+            if tick - 2 == HALF - 1:
+                gain_start()
+                gain_end()
         if 0 <= tick - 3 < HALF:
             hand_back(tick - 3)
+
+    gain_back()
+    gain_copy.wait()
+
+    @pl.when(ends)
+    def _():
+        for turn in range(1, shots):
+            pcopy(turn, shot).wait_send()
 
     for copy in exchange:
         copy.wait_send()
@@ -253,17 +313,19 @@
             def _():
                 for kind in range(2):
                     fcopy(d, h, kind, before).wait_send()
+                if h == 0:
+                    tcopy(d, before).wait_send()
 
 
 def local(queries, cotangent, ref_keys, ref_values, key_gain, owners, counts):
     tokens, width = queries.shape
     rows = ref_keys.shape[2]
-    chips = lax.axis_size("frame") // 2
+    shots, chips = lax.axis_size("shot"), lax.axis_size("frame") // 2
     vmem = pl.BlockSpec(memory_space=pltpu.VMEM)
     smem = pl.BlockSpec(memory_space=pltpu.SMEM)
     dma = pltpu.SemaphoreType.DMA
     gq, ok, ov, gain = pl.pallas_call(
-        functools.partial(kernel, chips),
+        functools.partial(kernel, shots, chips),
         out_shape=(
             jax.ShapeDtypeStruct((tokens, width), BF16),
             jax.ShapeDtypeStruct((rows, width), BF16),
@@ -284,19 +346,24 @@
             pltpu.VMEM((2, HALF, 2, rows, DH), BF16),
             pltpu.VMEM((HALF, 2, tokens, DH), BF16),
             pltpu.VMEM((HALF, 2, rows, DH), BF16),
+            pltpu.VMEM((shots, 8, WIDE), F32),
+            pltpu.VMEM((2, 8, WIDE), F32),
+            pltpu.VMEM((1, WIDE), F32),
             dma((4,)), dma((4,)),
             dma((2, HALF * 4)), dma((2, HALF * 4)),
             dma((2, HALF * 2)), dma((2, HALF * 2)),
             dma((2, HALF * 2)), dma((2, HALF * 2)),
             dma((HALF,)), dma((HALF,)),
             dma((HALF * 2,)), dma((HALF * 2,)),
+            dma((shots,)), dma((shots,)),
+            dma((2,)), dma((2,)),
+            dma((1,)), dma((1,)),
         ],
         compiler_params=pltpu.CompilerParams(
             collective_id=0, has_side_effects=True, vmem_limit_bytes=48 * 1024 * 1024
         ),
     )(owners[0], counts[0], queries, cotangent, ref_keys[0, 0], ref_values[0, 0], key_gain[None, :])
-    grad_gain = lax.psum(gain[0], ("shot", "frame"))
-    return gq, ok[None, None], ov[None, None], grad_gain
+    return gq, ok[None, None], ov[None, None], gain[0]
 
 
 def solution(mesh):

time: 146 us -> 116 us (0.79)
  blocking collectives: 38.9 us -> 0 us
  Pallas kernels: 98 us -> 107 us
    psum x1 -> x0, blocking collectives: 38.9 us -> none  [local(): grad_gain = lax.psum(gain[0], ('shot', 'frame'))]
    pallas_call x1, Pallas kernels: 98 us -> 107 us  [local(): pl.pallas_call(functools.partial(kernel, shots, chips), out_shape=(jax.Sh...]
where the time goes in v2:
time: 116 us
  Pallas kernels  107 us (92%)
  local copies, waits for them, and re-layouts  7.97 us (7%)
    pallas_call x1, Pallas kernels, local(): pl.pallas_call(functools.partial(kernel, shots, chips), out_shape=(jax.Sh...  107 us
    unnamed x17, local copies, waits for them, and re-layouts  7.97 us

profile of v2, /device:TPU:0, one launch (start us, length us, event | category | flops | bytes accessed | tf_op | source)
XLA Modules:
  0.0 115.8 jit_solution(1822068315211476792)
XLA Ops:
  0.6 0.0 copy-start.6
  0.6 0.7 copy-done.6
  1.3 0.0 copy-start.4
  1.3 0.0 copy-start.5
  1.3 0.6 copy-done.4
  2.0 0.0 copy-done.5
  2.0 0.0 copy-start
  2.0 1.1 copy-done
  3.1 0.0 copy-start.1
  3.1 1.1 copy-done.1
  4.3 0.0 copy-start.2
  4.3 1.0 copy-done.2
  5.3 0.0 copy-start.3
  5.3 1.0 copy-done.3
  6.3 106.6 %shard_map.102 = (bf16[512,768]{1,0:T(8,128)(2,1)S(1)}, bf16[256,768]{1,0:T(8,128)(2,1)S(1)}, bf16[256,768]{1,0:T(8,128)(2,1)S(1)}, f32[1,768]{1,0:T(1,128)S(1)}) custom-call(s32[2]{0:T(128)S(1)} %bitcast.10, s32[2]{0:T(128)S(1)} %bitcast.11, bf16[512,768]{1,0:T(8,128)(2,1)S(1)} %copy-done, bf16[512,768]{1,0:T(8,128)(2,1)S(1)} %copy-done.1, ...), custom_call_target="tpu_custom_call" | custom-call | tf_op jit(solution)/shard_map/pallas_call | solution.py:327
  112.8 0.6 reduce
  113.4 0.9 copy.14
  114.3 0.7 copy.15
  115.0 0.7 copy.16
  (1 shorter events, 0.0 us)
Async XLA Ops:
  0.6 0.7 copy-start.6
  1.3 0.7 copy-start.4
  1.3 0.7 copy-start.5
  2.0 1.1 copy-start
  3.1 1.1 copy-start.1
  4.3 1.0 copy-start.2
  5.3 1.0 copy-start.3

commit v3 on v2

--- a/solution.py
+++ b/solution.py
@@ -163,18 +163,39 @@
         gain_out[:, mine_cols] = gmine[...]
         gain_copy.start()
 
-    def spread(h):
-        for turn in range(2):
-            d = far if turn == 0 else 1 - far
-            pos, after, _ = way(d)
+    def near(turn):
+        return far if turn == 0 else 1 - far
+
+    def put(d, h, kv, j, first):
+        pos, after, _ = way(d)
+        here = lax.select(own[j] == me, (rk, rv)[kv][:, cols(h)], pkv[kv, :, h * DH : (h + 1) * DH])
+        if first:
+            buf[d, h, kv, j] = here
+            bcopy(d, h, kv, j, after).start()
+        else:
+            copy = bcopy(d, h, kv, j, after)
+            copy.wait_recv()
+            use = (own[j] >= 2 * z) & (own[j] < 2 * z + 2)
+            buf[d, h, kv, j] = lax.select(use, here, buf[d, h, kv, j])
+            pl.when(pos < last)(copy.start)
+
+    def spread_first():
+        @pl.when(ends)
+        def _():
+            for h in range(HALF):
+                for kv in range(2):
+                    for j in range(2):
+                        put(near(0), h, kv, j, True)
+
+    def spread(h, turn):
+        d = near(turn)
+        pos, _, _ = way(d)
+
+        @pl.when(pos > 0)
+        def _():
             for kv in range(2):
                 for j in range(2):
-                    copy = bcopy(d, h, kv, j, after)
-                    pl.when(pos > 0)(copy.wait_recv)
-                    here = lax.select(own[j] == me, (rk, rv)[kv][:, cols(h)], pkv[kv, :, h * DH : (h + 1) * DH])
-                    use = ((own[j] >= 2 * z) & (own[j] < 2 * z + 2)) | (pos == 0)
-                    buf[d, h, kv, j] = lax.select(use, here, buf[d, h, kv, j])
-                    pl.when(pos < last)(copy.start)
+                    put(d, h, kv, j, False)
 
     def raw(h, kv, j, owner):
         return lax.select(owner < 2 * z + 2, buf[0, h, kv, j], buf[1, h, kv, j])
@@ -238,32 +259,31 @@
             parts[shot, :, h * DH : (h + 1) * DH] = terms
         fcopy(d, h, kind, before).start()
 
-    def reduce(h):
-        for turn in range(2):
-            d = far if turn == 0 else 1 - far
-            pos, after, before = way(d)
-
-            @pl.when(pos > 0)
-            def _():
-                for kind in range(2):
-                    copy = rcopy(d, h, kind, after)
-                    copy.wait_recv()
-                    acc[h, kind, d] += rbuf[d, h, kind]
-                    pl.when(pos < last)(copy.start)
-                    pl.when(pos == last)(functools.partial(finish, d, h, kind, before))
-
-    def hand_back(h):
-        for turn in range(2):
-            d = 1 - far if turn == 0 else far
-            pos, _, before = way(d)
-
-            @pl.when(pos < last)
-            def _():
-                for kind in range(2):
-                    copy = fcopy(d, h, kind, before)
-                    copy.wait_recv()
-                    pl.when(pos > 0)(copy.start)
-
+    def reduce(h, turn):
+        d = near(turn)
+        pos, after, before = way(d)
+
+        @pl.when(pos > 0)
+        def _():
+            for kind in range(2):
+                copy = rcopy(d, h, kind, after)
+                copy.wait_recv()
+                acc[h, kind, d] += rbuf[d, h, kind]
+                pl.when(pos < last)(copy.start)
+                pl.when(pos == last)(functools.partial(finish, d, h, kind, before))
+
+    def hand_back(h, turn):
+        d = near(1 - turn)
+        pos, _, before = way(d)
+
+        @pl.when(pos < last)
+        def _():
+            for kind in range(2):
+                copy = fcopy(d, h, kind, before)
+                copy.wait_recv()
+                pl.when(pos > 0)(copy.start)
+
+    def hand_out(h):
         for kind in range(2):
             first, second = fin[0, h, kind], fin[1, h, kind]
             nothing = jnp.zeros_like(first)
@@ -272,18 +292,33 @@
             outs[h, kind] = lax.select(own[0] == peer, first, lax.select(own[1] == peer, second, nothing))
             ocopy(h, kind).start()
 
-    for tick in range(HALF + 4):
-        if tick < HALF:
-            spread(tick)
-        if 0 <= tick - 1 < HALF:
-            attend(tick - 1)
-        if 0 <= tick - 2 < HALF:
-            reduce(tick - 2)
-            if tick - 2 == HALF - 1:
-                gain_start()
-                gain_end()
-        if 0 <= tick - 3 < HALF:
-            hand_back(tick - 3)
+    n = HALF
+    spread_first()
+    spread(0, 0)
+    for h in range(n):
+        if h + 1 < n:
+            spread(h + 1, 0)
+        spread(h, 1)
+        if h > 0:
+            attend(h - 1)
+        if h > 1:
+            reduce(h - 2, 0)
+    attend(n - 1)
+    reduce(n - 2, 0)
+    reduce(0, 1)
+    reduce(n - 1, 0)
+    for h in range(1, n):
+        reduce(h, 1)
+        hand_back(h - 1, 0)
+        if h == n - 1:
+            gain_start()
+    for h in range(1, n):
+        hand_back(h - 1, 1)
+        hand_out(h - 1)
+    hand_back(n - 1, 0)
+    gain_end()
+    hand_back(n - 1, 1)
+    hand_out(n - 1)
 
     gain_back()
     gain_copy.wait()

time: 116 us -> 96.6 us (0.83)
  Pallas kernels: 107 us -> 87 us
    pallas_call x1, Pallas kernels: 107 us -> 87 us  [local(): pl.pallas_call(functools.partial(kernel, shots, chips), out_shape=(jax.Sh...]
where the time goes in v3:
time: 96.6 us; the launch traced here: 96.2 us
  Pallas kernels  87 us (90%)
  local copies, waits for them, and re-layouts  7.97 us (8%)
    pallas_call x1, Pallas kernels, local(): pl.pallas_call(functools.partial(kernel, shots, chips), out_shape=(jax.Sh...  87 us
    unnamed x17, local copies, waits for them, and re-layouts  7.97 us

profile of v3, /device:TPU:0, one launch (start us, length us, event | category | flops | bytes accessed | tf_op | source)
XLA Modules:
  0.0 96.2 jit_solution(14832282318695586941)
XLA Ops:
  0.6 0.0 copy-start.6
  0.6 0.7 copy-done.6
  1.3 0.0 copy-start.4
  1.3 0.0 copy-start.5
  1.3 0.6 copy-done.4
  2.0 0.0 copy-done.5
  2.0 0.0 copy-start
  2.0 1.1 %copy-done = bf16[512,768]{1,0:T(8,128)(2,1)S(1)} copy-done((bf16[512,768]{1,0:T(8,128)(2,1)S(1)}, bf16[512,768]{1,0:T(8,128)(2,1)}, u32[]{:S(2)}) %copy-start) | copy-done | bytes 786456
  3.1 0.0 copy-start.1
  3.1 1.1 %copy-done.1 = bf16[512,768]{1,0:T(8,128)(2,1)S(1)} copy-done((bf16[512,768]{1,0:T(8,128)(2,1)S(1)}, bf16[512,768]{1,0:T(8,128)(2,1)}, u32[]{:S(2)}) %copy-start.1) | copy-done | bytes 786456
  4.3 0.0 copy-start.2
  4.3 1.0 %copy-done.2 = bf16[1,1,256,768]{3,2,1,0:T(8,128)(2,1)S(1)} copy-done((bf16[1,1,256,768]{3,2,1,0:T(8,128)(2,1)S(1)}, bf16[1,1,256,768]{3,2,1,0:T(8,128)(2,1)}, u32[]{:S(2)}) %copy-start.2) | copy-done | bytes 393240
  5.3 0.0 copy-start.3
  5.3 1.0 %copy-done.3 = bf16[1,1,256,768]{3,2,1,0:T(8,128)(2,1)S(1)} copy-done((bf16[1,1,256,768]{3,2,1,0:T(8,128)(2,1)S(1)}, bf16[1,1,256,768]{3,2,1,0:T(8,128)(2,1)}, u32[]{:S(2)}) %copy-start.3) | copy-done | bytes 393240
  6.3 87.0 %shard_map.102 = (bf16[512,768]{1,0:T(8,128)(2,1)S(1)}, bf16[256,768]{1,0:T(8,128)(2,1)S(1)}, bf16[256,768]{1,0:T(8,128)(2,1)S(1)}, f32[1,768]{1,0:T(1,128)S(1)}) custom-call(s32[2]{0:T(128)S(1)} %bitcast.10, s32[2]{0:T(128)S(1)} %bitcast.11, bf16[512,768]{1,0:T(8,128)(2,1)S(1)} %copy-done, bf16[512,768]{1,0:T(8,128)(2,1)S(1)} %copy-done.1, ...), custom_call_target="tpu_custom_call" | custom-call | tf_op jit(solution)/shard_map/pallas_call | solution.py:362
  93.3 0.6 reduce
  93.9 0.9 copy.14
  94.8 0.7 copy.15
  95.5 0.7 copy.16
  (1 shorter events, 0.0 us)
Async XLA Ops:
  0.6 0.7 copy-start.6
  1.3 0.7 copy-start.4
  1.3 0.7 copy-start.5
  2.0 1.1 %copy-start = (bf16[512,768]{1,0:T(8,128)(2,1)S(1)}, bf16[512,768]{1,0:T(8,128)(2,1)}, u32[]{:S(2)}) copy-start(bf16[512,768]{1,0:T(8,128)(2,1)} %q.1) | copy-start | bytes 2359300
  3.1 1.1 %copy-start.1 = (bf16[512,768]{1,0:T(8,128)(2,1)S(1)}, bf16[512,768]{1,0:T(8,128)(2,1)}, u32[]{:S(2)}) copy-start(bf16[512,768]{1,0:T(8,128)(2,1)} %g.1) | copy-start | bytes 2359300
  4.3 1.0 %copy-start.2 = (bf16[1,1,256,768]{3,2,1,0:T(8,128)(2,1)S(1)}, bf16[1,1,256,768]{3,2,1,0:T(8,128)(2,1)}, u32[]{:S(2)}) copy-start(bf16[1,1,256,768]{3,2,1,0:T(8,128)(2,1)} %param.9) | copy-start | bytes 1179652
  5.3 1.0 %copy-start.3 = (bf16[1,1,256,768]{3,2,1,0:T(8,128)(2,1)S(1)}, bf16[1,1,256,768]{3,2,1,0:T(8,128)(2,1)}, u32[]{:S(2)}) copy-start(bf16[1,1,256,768]{3,2,1,0:T(8,128)(2,1)} %param.10) | copy-start | bytes 1179652

commit v4 on v3

--- a/solution.py
+++ b/solution.py
@@ -24,8 +24,8 @@
 def kernel(
     shots, chips, owners, counts, q, g, rk, rv, gain,
     gq_out, ok_out, ov_out, gain_out,
-    qh, gh, pkv, buf, kn, vn, acc, rbuf, fin, gqs, outs, parts, gsum, gmine,
-    xs, xr, bs, br, rs, rr, fs, fr, gs, gr, os_, or_, ps, pr, ts, tr, ms, mr,
+    qh, gh, pkv, buf, kn, vn, acc, rbuf, fin, gqs, outs, parts, gsum, gmine, okv,
+    xs, xr, bs, br, rs, rr, fs, fr, gs, gr, os_, or_, ps, pr, ts, tr, ms, mr, ls,
 ):
     shot = lax.axis_index("shot")
     me = lax.axis_index("frame")
@@ -45,6 +45,17 @@
             device_id=dev(frame), device_id_type=pl.DeviceIdType.MESH,
         )
 
+    base = core * WIDE
+    mine_cols = pl.ds(pl.multiple_of(base, DH), WIDE)
+    fetch = [
+        pltpu.make_async_copy(rk.at[:, mine_cols], okv.at[0], ls.at[0]),
+        pltpu.make_async_copy(rv.at[:, mine_cols], okv.at[1], ls.at[1]),
+        pltpu.make_async_copy(q.at[:, mine_cols], qh.at[core], ls.at[2]),
+        pltpu.make_async_copy(g.at[:, mine_cols], gh.at[core], ls.at[3]),
+    ]
+    for copy in fetch:
+        copy.start()
+
     barrier = pltpu.get_barrier_semaphore()
     pl.semaphore_signal(barrier, inc=1, device_id=dev(peer), device_id_type=pl.DeviceIdType.MESH)
 
@@ -63,12 +74,10 @@
 
     own = [owners[0], owners[1]]
     far = (z * 2 >= chips).astype(jnp.int32)
-    base = core * WIDE
 
     def cols(h):
         return pl.ds(pl.multiple_of(base + h * DH, DH), DH)
 
-    mine_cols = pl.ds(pl.multiple_of(base, DH), WIDE)
     peer_cols = pl.ds(pl.multiple_of((1 - core) * WIDE, DH), WIDE)
 
     def way(d):
@@ -90,8 +99,8 @@
     ]
     for copy in exchange:
         copy.start()
-    qh[core] = q[:, mine_cols]
-    gh[core] = g[:, mine_cols]
+    fetch[0].wait()
+    fetch[1].wait()
     landing[0].wait_recv()
     landing[1].wait_recv()
 
@@ -168,7 +177,7 @@
 
     def put(d, h, kv, j, first):
         pos, after, _ = way(d)
-        here = lax.select(own[j] == me, (rk, rv)[kv][:, cols(h)], pkv[kv, :, h * DH : (h + 1) * DH])
+        here = lax.select(own[j] == me, okv[kv, :, h * DH : (h + 1) * DH], pkv[kv, :, h * DH : (h + 1) * DH])
         if first:
             buf[d, h, kv, j] = here
             bcopy(d, h, kv, j, after).start()
@@ -214,6 +223,8 @@
             kn[j * rows : (j + 1) * rows] = (unit * gain[:, cols(h)]).astype(BF16)
             vn[j * rows : (j + 1) * rows] = raw(h, 1, j, own[j])
         if h == 0:
+            fetch[2].wait()
+            fetch[3].wait()
             landing[2].wait_recv()
             landing[3].wait_recv()
         acc[h] = jnp.zeros_like(acc[h])
@@ -299,12 +310,9 @@
         if h + 1 < n:
             spread(h + 1, 0)
         spread(h, 1)
+        attend(h)
         if h > 0:
-            attend(h - 1)
-        if h > 1:
-            reduce(h - 2, 0)
-    attend(n - 1)
-    reduce(n - 2, 0)
+            reduce(h - 1, 0)
     reduce(0, 1)
     reduce(n - 1, 0)
     for h in range(1, n):
@@ -367,7 +375,7 @@
             jax.ShapeDtypeStruct((rows, width), BF16),
             jax.ShapeDtypeStruct((1, width), F32),
         ),
-        in_specs=[smem, smem] + [vmem] * 5,
+        in_specs=[smem, smem] + [pl.BlockSpec(memory_space=pl.ANY)] * 4 + [vmem],
         out_specs=(vmem,) * 4,
         scratch_shapes=[
             pltpu.VMEM((2, tokens, WIDE), BF16),
@@ -384,6 +392,7 @@
             pltpu.VMEM((shots, 8, WIDE), F32),
             pltpu.VMEM((2, 8, WIDE), F32),
             pltpu.VMEM((1, WIDE), F32),
+            pltpu.VMEM((2, rows, WIDE), BF16),
             dma((4,)), dma((4,)),
             dma((2, HALF * 4)), dma((2, HALF * 4)),
             dma((2, HALF * 2)), dma((2, HALF * 2)),
@@ -393,9 +402,10 @@
             dma((shots,)), dma((shots,)),
             dma((2,)), dma((2,)),
             dma((1,)), dma((1,)),
+            dma((4,)),
         ],
         compiler_params=pltpu.CompilerParams(
-            collective_id=0, has_side_effects=True, vmem_limit_bytes=48 * 1024 * 1024
+            collective_id=0, has_side_effects=True, vmem_limit_bytes=60 * 1024 * 1024
         ),
     )(owners[0], counts[0], queries, cotangent, ref_keys[0, 0], ref_values[0, 0], key_gain[None, :])
     return gq, ok[None, None], ov[None, None], gain[0]

time: 96.6 us -> 95.4 us (0.988)
  local copies, waits for them, and re-layouts: 7.97 us -> 5.93 us
    unnamed x17 -> x11, local copies, waits for them, and re-layouts: 7.97 us -> 5.35 us
where the time goes in v4:
time: 95.4 us; the launch traced here: 95.1 us
  Pallas kernels  87.9 us (92%)
  local copies, waits for them, and re-layouts  5.93 us (6%)
    pallas_call x1, Pallas kernels, local(): pl.pallas_call(functools.partial(kernel, shots, chips), out_shape=(jax.Sh...  87.9 us
    unnamed x11, local copies, waits for them, and re-layouts  5.35 us

profile of v4, /device:TPU:0, one launch (start us, length us, event | category | flops | bytes accessed | tf_op | source)
XLA Modules:
  0.0 95.1 jit_solution(9365337348530222535)
XLA Ops:
  0.6 0.0 copy-start.2
  0.6 0.7 copy-done.2
  1.3 0.6 broadcast_in_dim.9.gain
  1.9 87.9 %shard_map.102 = (bf16[512,768]{1,0:T(8,128)(2,1)}, bf16[256,768]{1,0:T(8,128)(2,1)}, bf16[256,768]{1,0:T(8,128)(2,1)}, f32[1,768]{1,0:T(1,128)}) custom-call(s32[2]{0:T(128)} %bitcast.10, s32[2]{0:T(128)} %bitcast.11, bf16[512,768]{1,0:T(8,128)(2,1)} %q.1, bf16[512,768]{1,0:T(8,128)(2,1)} %g.1, bf16[256,768]{1,0:T(8,128)(2,1)} %bitcast.6, ...), custom_call_target="tpu_custom_call" | custom-call | tf_op jit(solution)/shard_map/pallas_call | solution.py:370
  89.8 0.0 copy-start.3
  89.8 0.7 copy-done.3
  90.5 0.6 reduce
  91.1 0.0 copy-start.1
  91.1 2.1 %copy.14 = bf16[512,768]{1,0:T(8,128)(2,1)} copy(bf16[512,768]{1,0:T(8,128)(2,1)} %get-tuple-element.16) | data formatting | bytes 1572864
  93.2 0.0 copy-done.1
  93.2 0.0 copy-start
  93.2 0.7 copy.15
  94.0 0.4 copy-done
  94.3 0.7 copy.16
Async XLA Ops:
  0.6 0.7 copy-start.2
  89.8 0.7 copy-start.3
  91.1 2.1 %copy-start.1 = (bf16[256,768]{1,0:T(8,128)(2,1)S(1)}, bf16[256,768]{1,0:T(8,128)(2,1)}, u32[]{:S(2)}) copy-start(bf16[256,768]{1,0:T(8,128)(2,1)} %get-tuple-element.9) | copy-start | bytes 1179652
  93.2 1.1 %copy-start = (bf16[256,768]{1,0:T(8,128)(2,1)S(1)}, bf16[256,768]{1,0:T(8,128)(2,1)}, u32[]{:S(2)}) copy-start(bf16[256,768]{1,0:T(8,128)(2,1)} %get-tuple-element.10) | copy-start | bytes 1179652
